TPU v7x, 256 devices: a whole 4x4x8 slice. The times are simulated.
256 devices in a mesh: oi: 16 (over z, x_lo), oj: 8 (over y, core), vert: 2 (over x_hi).
Axes of the slice: x: 4 (x_hi: 2, x_lo: 2; x = x_hi * 2 + x_lo), y: 4, z: 8, core: 2. Of those that a mesh axis runs over, the one named last changes fastest.
Arguments:
- amplitudes: bfloat16 [16, 16, 1200, 1200], P('oi', 'oj'), may hold values from -0.23925781 to 0.23925781
- slabs: bfloat16 [4, 1200, 300], P(None, 'oi'), may hold values from -0.375 to 0.375
- occ_bins: int32 [16], replicated, may hold values from 0 to 63
- vir_bins: int32 [4], replicated, may hold values from 0 to 63
- occ_levels: float32 [64], replicated, may hold values from -2 to -0.3
- vir_levels: float32 [64], replicated, may hold values from 0.2 to 3
Outputs:
- amps_new: float32 [16, 16, 4, 4], P('oi', 'oj', 'vert')
- doubled: bfloat16 [16, 16, 4, 4], P('oi', 'oj', 'vert')
All inputs are finite; a program needn't handle non-finite values.
Results may differ from a plain program's by a relative error of at most 0.01.
Values may be sent and summed in bfloat16 or wider, within the bound.
A program may use at most 128 MiB of HBM per device.

v0:
```python
import jax
import jax.numpy as jnp
from jax import lax
from jax.experimental import pallas as pl
from jax.experimental.pallas import tpu as pltpu
from jax.sharding import PartitionSpec as P

MESH = pl.DeviceIdType.MESH
LANES = 128
N_Z = 8
TAIL = 32
ORDER = (1, 7, 2, 6, 3, 5, 4)
GROUPS = ((0, 5), (5, 8))


def place_of(r):
    far = r // 5
    return (1 - far) * (2 * r - 1) + far * (16 - 2 * r) + (8 - r) // 8


def kernel(amps, slabs, occ_bins, vir_bins, occ_levels, vir_levels, out_new, out_two,
           t, own, ra, rb, rc, bf, bc, y, acc, mine, from_vert, from_pair,
           t_sem, own_sem, zs, zr, xs, xr, cs, cr, fs, fr):
    oi, oj, v = lax.axis_index("oi"), lax.axis_index("oj"), lax.axis_index("vert")
    z, xl, yy, c = oi // 2, oi % 2, oj // 2, oj % 2
    virt, full, aux = own.shape[0], amps.shape[2], own.shape[2]
    span = own.shape[1]
    bufs = (ra, rb, rc)

    own_copy = pltpu.make_async_copy(slabs, own, own_sem)
    own_copy.start()
    t_copies = []
    for p in range(2):
        cp = pltpu.make_async_copy(amps.at[0, p], t.at[p], t_sem.at[p])
        cp.start()
        t_copies.append(cp)

    def ring(d):
        return (lax.rem(z + d, N_Z) * 2 + xl, oj, v)

    across = (z * 2 + 1 - xl, oj, v)
    sibling = (oi, yy * 2 + 1 - c, v)
    peer = (oi, oj, 1 - v)
    diag = [(oj * 2 + p) == oi for p in range(2)]

    def pair(p, w):
        return (oj * 2 + p, oi // 2, w)

    barrier = pltpu.get_barrier_semaphore()
    for d in ORDER:
        pl.semaphore_signal(barrier, inc=1, device_id=ring(d), device_id_type=MESH)
    for who in (across, sibling, peer):
        pl.semaphore_signal(barrier, inc=1, device_id=who, device_id_type=MESH)
    for p in range(2):
        for dv in range(2):
            if dv == 1:
                pl.semaphore_signal(barrier, inc=1, device_id=pair(p, 1 - v), device_id_type=MESH)
            else:
                @pl.when(jnp.logical_not(diag[p]))
                def _(p=p):
                    pl.semaphore_signal(barrier, inc=1, device_id=pair(p, v), device_id_type=MESH)

    own_copy.wait()
    lane = lax.broadcasted_iota(jnp.int32, (80, LANES), 1)
    left = aux - 2 * LANES
    half_left = left // 2
    tail = jnp.zeros((80, LANES), jnp.float32)
    for a in range(virt):
        rows = own[a].astype(jnp.float32)
        rows = jnp.concatenate([rows, jnp.zeros((80 - span, aux), jnp.float32)], axis=0)
        main = jnp.where(v == 0, rows[:, :LANES], rows[:, LANES : 2 * LANES])
        bufs[a // 2][a % 2, xl, 0] = main.astype(jnp.bfloat16)
        rest = jnp.concatenate([rows[:, 2 * LANES :], jnp.zeros((80, LANES - left), jnp.float32)], axis=1)
        first = pltpu.roll(rest, TAIL * a, 1) if a else rest
        second = pltpu.roll(rest, (TAIL * a - half_left) % LANES, 1)
        moved = jnp.where(v == 0, first, second)
        tail = jnp.where((lane >= TAIL * a) & (lane < TAIL * a + half_left), moved, tail)
    rc[0, xl, 0] = tail[:48].astype(jnp.bfloat16)
    rc[1, xl, 0] = jnp.concatenate([tail[48:], jnp.zeros((16, LANES), jnp.float32)], axis=0).astype(jnp.bfloat16)

    is_diag = diag[0].astype(jnp.int32) + diag[1].astype(jnp.int32)
    pl.semaphore_wait(barrier, 14 - is_diag)

    def remote(src, dst, s, r, who):
        cp = pltpu.make_async_remote_copy(
            src_ref=src, dst_ref=dst, send_sem=s, recv_sem=r, device_id=who, device_id_type=MESH)
        cp.start()
        return cp

    sent = []
    z_copies = []
    for n, buf in enumerate(bufs):
        row = {}
        for d in ORDER:
            row[d] = remote(buf.at[c, xl, 0], buf.at[c, xl, place_of(N_Z - d)], zs.at[n, d - 1], zr.at[n, d - 1], ring(d))
            sent.append(row[d])
        z_copies.append(row)

    x_copies = [[None, None] for _ in bufs]
    c_copies = [[None] * 4 for _ in bufs]

    def after_z(n):
        buf = bufs[n]
        for g, (lo, hi) in enumerate(GROUPS):
            for d in ORDER:
                if lo <= place_of(N_Z - d) < hi:
                    z_copies[n][d].wait_recv()
            block = buf.at[c, xl, pl.ds(lo, hi - lo)]
            x_copies[n][g] = remote(block, block, xs.at[n, g], xr.at[n, g], across)
            lo = max(lo, 1)
            block = buf.at[c, xl, pl.ds(lo, hi - lo)]
            c_copies[n][g] = remote(block, block, cs.at[n, g], cr.at[n, g], sibling)
            sent.extend([x_copies[n][g], c_copies[n][g]])

    def after_x(n):
        buf = bufs[n]
        for g, (lo, hi) in enumerate(GROUPS):
            x_copies[n][g].wait_recv()
            block = buf.at[c, 1 - xl, pl.ds(lo, hi - lo)]
            c_copies[n][2 + g] = remote(block, block, cs.at[n, 2 + g], cr.at[n, 2 + g], sibling)
            sent.append(c_copies[n][2 + g])

    def after_c(n):
        for cp in c_copies[n]:
            cp.wait_recv()
        buf = bufs[n]
        for zz in range(N_Z):
            pos = place_of(lax.rem(zz - z + N_Z, N_Z))
            for half in range(2):
                at = (2 * zz + half) * span
                if n < 2:
                    for k in range(2):
                        bf[2 * n + k, at : at + span, :] = buf[k, half, pos][:span].astype(jnp.float32)
                else:
                    bf[4, at : at + 48, :] = buf[0, half, pos].astype(jnp.float32)
                    bf[4, at + 48 : at + span, :] = buf[1, half, pos][: span - 48].astype(jnp.float32)
        for a in range(2 * n, min(2 * n + 2, 5)):
            bc[:, LANES * a : LANES * (a + 1)] = bf[a].astype(jnp.bfloat16)

    def multiply(n):
        cols = slice(256 * n, min(256 * n + 256, 5 * LANES))
        for p in range(2):
            y[p, :, cols] = jnp.dot(t[p], bc[:, cols], preferred_element_type=jnp.float32)

    step = 80

    def fold(x):
        return jnp.sum(x.reshape(step // 8, 8, LANES), axis=0)

    after_z(0)
    after_z(1)
    after_x(0)
    after_z(2)
    after_x(1)
    acc[...] = jnp.zeros_like(acc)
    after_c(0)
    for cp in t_copies:
        cp.wait()
    multiply(0)
    after_x(2)
    after_c(1)
    multiply(1)

    @pl.loop(0, full // step)
    def _(s):
        rows = pl.ds(pl.multiple_of(s * step, 16), step)
        fac = [bf[a, rows, :] for a in range(4)]
        for p in range(2):
            for b in range(4):
                part = y[p, rows, LANES * b : LANES * (b + 1)]
                for a in range(4):
                    acc[p, a, b] += fold(part * fac[a])

    after_c(2)
    multiply(2)

    @pl.loop(0, full // step)
    def _(s):
        rows = pl.ds(pl.multiple_of(s * step, 16), step)
        fac = bf[4, rows, :]
        turned = [fac] + [pltpu.roll(fac, TAIL * d, 1) for d in range(1, 4)]
        for p in range(2):
            part = y[p, rows, 4 * LANES : 5 * LANES]
            for d in range(4):
                acc[p, 4, d] += fold(part * turned[d])

    lane = lax.broadcasted_iota(jnp.int32, (8, LANES), 1)
    for p in range(2):
        for a in range(4):
            for b in range(4):
                inside = (lane >= TAIL * b) & (lane < TAIL * (b + 1))
                total = acc[p, a, b] + jnp.where(inside, acc[p, 4, (b - a) % 4], 0.0)
                total = jnp.sum(total, axis=0, keepdims=True)
                mine[p, 4 * a + b : 4 * a + b + 1, :] = total
                mine[p, 16 + 4 * b + a : 16 + 4 * b + a + 1, :] = total
    for p in range(2):
        mine[p] = jnp.broadcast_to(jnp.sum(mine[p], axis=1, keepdims=True), (32, LANES))

    place = oi % 2
    to_vert = remote(mine, from_vert, fs.at[4], fr.at[2, 0], peer)
    sent.append(to_vert)
    for p in range(2):
        remote(mine.at[p], from_pair.at[place, v], fs.at[2 * p + 1], fr.at[place, v], pair(p, 1 - v))

        @pl.when(jnp.logical_not(diag[p]))
        def _(p=p):
            remote(mine.at[p], from_pair.at[place, v], fs.at[2 * p], fr.at[place, v], pair(p, v))

        @pl.when(diag[p])
        def _(p=p):
            pltpu.make_async_copy(mine.at[p], from_pair.at[p, v], fr.at[p, v]).start()

    row = lax.broadcasted_iota(jnp.int32, (16, LANES), 0)
    energy_i = occ_levels[occ_bins[oi]]
    ea = jnp.zeros((16, LANES), jnp.float32)
    eb = jnp.zeros((16, LANES), jnp.float32)
    for k in range(4):
        level = vir_levels[vir_bins[k]]
        ea = jnp.where(row // 4 == k, level, ea)
        eb = jnp.where(row % 4 == k, level, eb)

    to_vert.wait_recv()
    for p in range(2):
        for w in range(2):
            pltpu.make_async_copy(from_pair.at[p, w], from_pair.at[p, w], fr.at[p, w]).wait()
        here = mine[p] + from_vert[p]
        there = from_pair[p, 0] + from_pair[p, 1]
        denom = energy_i + occ_levels[occ_bins[oj * 2 + p]] - ea - eb
        new = (here[:16] + there[16:]) / denom
        swapped = (there[:16] + here[16:]) / denom
        two = 2.0 * new - swapped
        new = jnp.where(v == 0, new[:8], new[8:])
        two = jnp.where(v == 0, two[:8], two[8:])
        keep = lane == lax.broadcasted_iota(jnp.int32, (8, LANES), 0) % 4

        def spread(x):
            x = jnp.where(keep, x, 0.0)
            return jnp.concatenate(
                [jnp.sum(x[:4], axis=0, keepdims=True), jnp.sum(x[4:], axis=0, keepdims=True)], axis=0)[:, :4]

        out_new[0, p] = spread(new)
        out_two[0, p] = spread(two).astype(jnp.bfloat16)

    for cp in sent:
        cp.wait_send()
    for p in range(2):
        pltpu.make_async_copy(mine.at[p], mine.at[p], fs.at[2 * p + 1]).wait()

        @pl.when(jnp.logical_not(diag[p]))
        def _(p=p):
            pltpu.make_async_copy(mine.at[p], mine.at[p], fs.at[2 * p]).wait()


def on_device(amplitudes, slabs, occ_bins, vir_bins, occ_levels, vir_levels):
    full = amplitudes.shape[2]
    bf16, f32 = jnp.bfloat16, jnp.float32
    dma, vmem = pltpu.SemaphoreType.DMA, pltpu.VMEM
    any_space = pl.BlockSpec(memory_space=pl.ANY)
    smem = pl.BlockSpec(memory_space=pltpu.SMEM)
    return pl.pallas_call(
        kernel,
        out_shape=(jax.ShapeDtypeStruct((1, 2, 2, 4), f32), jax.ShapeDtypeStruct((1, 2, 2, 4), bf16)),
        in_specs=[any_space, any_space, smem, smem, smem, smem],
        out_specs=(pl.BlockSpec(memory_space=pltpu.VMEM), pl.BlockSpec(memory_space=pltpu.VMEM)),
        scratch_shapes=[
            vmem((2, full, full), bf16),
            vmem(slabs.shape, bf16),
            vmem((2, 2, N_Z, 80, LANES), bf16),
            vmem((2, 2, N_Z, 80, LANES), bf16),
            vmem((2, 2, N_Z, 48, LANES), bf16),
            vmem((5, full, LANES), f32),
            vmem((full, 5 * LANES), bf16),
            vmem((2, full, 5 * LANES), f32),
            vmem((2, 5, 4, 8, LANES), f32),
            vmem((2, 32, LANES), f32),
            vmem((2, 32, LANES), f32),
            vmem((2, 2, 32, LANES), f32),
            dma((2,)), dma,
            dma((3, 7)), dma((3, 7)),
            dma((3, 2)), dma((3, 2)),
            dma((3, 4)), dma((3, 4)),
            dma((5,)), dma((3, 2)),
        ],
        compiler_params=pltpu.CompilerParams(
            collective_id=0, has_side_effects=True, vmem_limit_bytes=48 << 20),
    )(amplitudes, slabs, occ_bins, vir_bins, occ_levels, vir_levels)


def solution(mesh):
    return jax.shard_map(
        on_device,
        mesh=mesh,
        in_specs=(P("oi", "oj", None, None), P(None, "oi", None), P(), P(), P(), P()),
        out_specs=(P("oi", "oj", "vert", None), P("oi", "oj", "vert", None)),
        check_vma=False,
    )
```

profile of v0, /device:TPU:16, one launch (start us, length us, event | category | flops | bytes accessed | tf_op | source)
XLA Modules:
  0.0 45.9 jit_solution(16606991128872721335)
XLA Ops:
  0.6 1.0 %copy.8.slabs = bf16[4,75,300]{2,1,0:T(8,128)(2,1)S(1)} copy(bf16[4,75,300]{2,0,1:T(4,128)(2,1)} %param.7) | data formatting | bytes 360000 | tf_op args[1]
  1.6 0.0 copy-start
  1.6 0.6 %copy-done = s32[16]{0:T(128)S(1)} copy-done((s32[16]{0:T(128)S(1)}, s32[16]{0:T(128)}, u32[]{:S(2)}) %copy-start) | copy-done | bytes 88
  2.3 0.0 copy-start.1
  2.3 0.7 %copy-done.1 = s32[4]{0:T(128)S(1)} copy-done((s32[4]{0:T(128)S(1)}, s32[4]{0:T(128)}, u32[]{:S(2)}) %copy-start.1) | copy-done | bytes 40
  2.9 0.0 copy-start.2
  2.9 0.7 %copy-done.2 = f32[64]{0:T(128)S(1)} copy-done((f32[64]{0:T(128)S(1)}, f32[64]{0:T(128)}, u32[]{:S(2)}) %copy-start.2) | copy-done | bytes 280
  3.6 0.0 copy-start.3
  3.6 0.7 %copy-done.3 = f32[64]{0:T(128)S(1)} copy-done((f32[64]{0:T(128)S(1)}, f32[64]{0:T(128)}, u32[]{:S(2)}) %copy-start.3) | copy-done | bytes 280
  4.2 40.5 %shard_map.77 = (f32[1,2,2,4]{3,2,1,0:T(2,128)S(1)}, bf16[1,2,2,4]{3,2,1,0:T(2,128)(2,1)S(1)}) custom-call(bf16[1,2,1200,1200]{3,2,1,0:T(8,128)(2,1)} %amps.1, bf16[4,75,300]{2,1,0:T(8,128)(2,1)S(1)} %copy.8.slabs, s32[16]{0:T(128)S(1)} %copy-done, s32[4]{0:T(128)S(1)} %copy-done.1, f32[64]{0:T(128)S(1)} %copy-done.2, f32[64]{0:T(128)S(1)} %copy-done.3), custom_call_target="tpu_custom_call" | custom-call | tf_op jit(solution)/shard_map/pallas_call | solution.py:260
  44.7 0.6 %copy.11 = f32[1,2,2,4]{3,2,1,0:T(2,128)} copy(f32[1,2,2,4]{3,2,1,0:T(2,128)S(1)} %get-tuple-element.4) | data formatting | bytes 128
  45.3 0.6 %copy.12 = bf16[1,2,2,4]{3,2,1,0:T(2,128)(2,1)} copy(bf16[1,2,2,4]{3,2,1,0:T(2,128)(2,1)S(1)} %get-tuple-element.5) | data formatting | bytes 64
Async XLA Ops:
  1.6 0.7 %copy-start = (s32[16]{0:T(128)S(1)}, s32[16]{0:T(128)}, u32[]{:S(2)}) copy-start(s32[16]{0:T(128)} %occ_bins.1) | copy-start | bytes 196
  2.3 0.7 %copy-start.1 = (s32[4]{0:T(128)S(1)}, s32[4]{0:T(128)}, u32[]{:S(2)}) copy-start(s32[4]{0:T(128)} %vir_bins.1) | copy-start | bytes 52
  2.9 0.7 %copy-start.2 = (f32[64]{0:T(128)S(1)}, f32[64]{0:T(128)}, u32[]{:S(2)}) copy-start(f32[64]{0:T(128)} %occ_levels.1) | copy-start | bytes 772
  3.6 0.7 %copy-start.3 = (f32[64]{0:T(128)S(1)}, f32[64]{0:T(128)}, u32[]{:S(2)}) copy-start(f32[64]{0:T(128)} %vir_levels.1) | copy-start | bytes 772
where the time goes:
time: 46 us; the launch traced here: 45.9 us
  Pallas kernels  40.5 us (88%)
  local copies, waits for them, and re-layouts  4.73 us (10%)
  between operations  0.65 us (1%)
    pallas_call x1, Pallas kernels, on_device(): pl.pallas_call(kernel, out_shape=(jax.ShapeDtypeStruct((1, 2, 2, 4), f32)...  40.5 us
    unnamed x11, local copies, waits for them, and re-layouts  4.73 us

commit v1 on v0

v1 whole, which is shorter than its diff:
```python
import jax
import jax.numpy as jnp
from jax import lax
from jax.experimental import pallas as pl
from jax.experimental.pallas import tpu as pltpu
from jax.sharding import PartitionSpec as P

MESH = pl.DeviceIdType.MESH
LANES = 128
N_Z = 8
TAIL = 32
EARLY = (False, False, True)
GROUPS = ((0, 1), (1, 5), (5, 8))
STEPS = (1, -1, 2, -2)


def place_of(r):
    far = r // 5
    return (1 - far) * (2 * r - 1) + far * (16 - 2 * r) + (8 - r) // 8


def kernel(amps, slabs, occ_bins_in, vir_bins_in, occ_levels_in, vir_levels_in, out,
           occ_bins, vir_bins, occ_levels, vir_levels, small_sem, t, own, ra, rb, rc, bf, bc, y, acc, mine, from_vert, from_pair,
           t_sem, own_sem, zs, zr, xs, xr, cs, cr, fs, fr):
    oi, oj, v = lax.axis_index("oi"), lax.axis_index("oj"), lax.axis_index("vert")
    z, xl, yy, c = oi // 2, oi % 2, oj // 2, oj % 2
    span, virt, aux = own.shape
    full = amps.shape[2]
    bufs = (ra, rb, rc)

    def ring(d, line):
        return (lax.rem(z + d + N_Z, N_Z) * 2 + line, oj, v)

    across = (z * 2 + 1 - xl, oj, v)
    sibling = (oi, yy * 2 + 1 - c, v)
    peer = (oi, oj, 1 - v)
    diag = [(oj * 2 + p) == oi for p in range(2)]

    def pair(p, w):
        return (oj * 2 + p, oi // 2, w)

    barrier = pltpu.get_barrier_semaphore()
    near = [ring(d, xl) for d in STEPS] + [across, sibling, peer]
    if any(EARLY):
        near += [ring(d, 1 - xl) for d in STEPS]
    for who in near:
        pl.semaphore_signal(barrier, inc=1, device_id=who, device_id_type=MESH)

    hub = oj == z
    for line in range(2):
        for w in range(2):
            @pl.when(jnp.logical_not(hub & (line == xl) & (w == v)))
            def _(line=line, w=w):
                pl.semaphore_signal(barrier, inc=1, device_id=(z * 2 + line, z, w), device_id_type=MESH)

    own_copy = pltpu.make_async_copy(slabs, own, own_sem)
    own_copy.start()
    small = []
    for k, (src, dst) in enumerate((
            (occ_bins_in, occ_bins), (vir_bins_in, vir_bins), (occ_levels_in, occ_levels), (vir_levels_in, vir_levels))):
        cp = pltpu.make_async_copy(src, dst, small_sem.at[k])
        cp.start()
        small.append(cp)
    t_copies = []
    for p in range(2):
        cp = pltpu.make_async_copy(amps.at[0, p], t.at[p], t_sem.at[p])
        cp.start()
        t_copies.append(cp)

    own_copy.wait()
    wide_own = own[...].astype(jnp.float32)
    lane = lax.broadcasted_iota(jnp.int32, (80, LANES), 1)
    left = aux - 2 * LANES
    half_left = left // 2
    tail = jnp.zeros((80, LANES), jnp.float32)
    for a in range(virt):
        rows = wide_own[:, a, :]
        rows = jnp.concatenate([rows, jnp.zeros((80 - span, aux), jnp.float32)], axis=0)
        main = jnp.where(v == 0, rows[:, :LANES], rows[:, LANES : 2 * LANES])
        bufs[a // 2][a % 2, xl, 0] = main.astype(jnp.bfloat16)
        rest = jnp.concatenate([rows[:, 2 * LANES :], jnp.zeros((80, LANES - left), jnp.float32)], axis=1)
        first = pltpu.roll(rest, TAIL * a, 1) if a else rest
        second = pltpu.roll(rest, (TAIL * a - half_left) % LANES, 1)
        moved = jnp.where(v == 0, first, second)
        tail = jnp.where((lane >= TAIL * a) & (lane < TAIL * a + half_left), moved, tail)
    rc[0, xl, 0] = tail[:48].astype(jnp.bfloat16)
    rc[1, xl, 0] = jnp.concatenate([tail[48:], jnp.zeros((16, LANES), jnp.float32)], axis=0).astype(jnp.bfloat16)

    pl.semaphore_wait(barrier, len(near) + 31 * hub.astype(jnp.int32))

    def remote(src, dst, s, r, who):
        cp = pltpu.make_async_remote_copy(
            src_ref=src, dst_ref=dst, send_sem=s, recv_sem=r, device_id=who, device_id_type=MESH)
        cp.start()
        return cp

    sent = []

    def send(src, dst, s, r, who):
        sent.append(remote(src, dst, s, r, who))
        return sent[-1]

    x_copies = [[None] * 3 for _ in bufs]
    c_copies = [[] for _ in bufs]
    z_first, z_second = [], []

    def to_sibling(n, block):
        k = len(c_copies[n])
        c_copies[n].append(send(block, block, cs.at[n, k], cr.at[n, k], sibling))

    def x_send(n, g):
        lo, hi = GROUPS[g]
        block = bufs[n].at[c, xl, pl.ds(lo, hi - lo)]
        x_copies[n][g] = send(block, block, xs.at[n, g], xr.at[n, g], across)

    def start(n):
        buf, row = bufs[n], []
        for k, d in enumerate(STEPS):
            row.append(send(buf.at[c, xl, 0], buf.at[c, xl, place_of(-d % N_Z)], zs.at[n, k], zr.at[n, k], ring(d, xl)))
        x_send(n, 0)
        if EARLY[n]:
            for k, d in enumerate(STEPS):
                row.append(send(
                    buf.at[c, xl, 0], buf.at[c, xl, place_of(-d % N_Z)], zs.at[n, 7 + k], zr.at[n, 7 + k], ring(d, 1 - xl)))
        z_first.append(row)

    def after_first(n):
        buf = bufs[n]
        for cp in z_first[n]:
            cp.wait_recv()
        lines = pl.ds(0, 2) if EARLY[n] else pl.ds(xl, 1)
        back, ahead = place_of(6), place_of(2)
        row = [
            send(buf.at[c, lines, back], buf.at[c, lines, place_of(5)], zs.at[n, 4], zr.at[n, 4], ring(1, xl)),
            send(buf.at[c, lines, ahead], buf.at[c, lines, place_of(3)], zs.at[n, 5], zr.at[n, 5], ring(-1, xl)),
            send(buf.at[c, lines, back + c * (ahead - back)], buf.at[c, lines, place_of(4)],
                 zs.at[n, 6], zr.at[n, 6], ring(2 - 4 * c, xl)),
        ]
        z_second.append(row)
        if not EARLY[n]:
            x_send(n, 1)
        to_sibling(n, buf.at[c, lines, pl.ds(1, 4)])

    def after_second(n):
        buf = bufs[n]
        for cp in z_second[n]:
            cp.wait_recv()
        lines = pl.ds(0, 2) if EARLY[n] else pl.ds(xl, 1)
        if not EARLY[n]:
            x_send(n, 2)
        to_sibling(n, buf.at[c, lines, pl.ds(5, 3)])

    def after_x(n, g):
        x_copies[n][g].wait_recv()
        lo, hi = GROUPS[g]
        to_sibling(n, bufs[n].at[c, 1 - xl, pl.ds(lo, hi - lo)])

    def after_c(n):
        for cp in c_copies[n]:
            cp.wait_recv()
        buf = bufs[n]
        for zz in range(N_Z):
            pos = place_of(lax.rem(zz - z + N_Z, N_Z))
            for half in range(2):
                at = (2 * zz + half) * span
                if n < 2:
                    for k in range(2):
                        bf[2 * n + k, at : at + span, :] = buf[k, half, pos][:span].astype(jnp.float32)
                else:
                    bf[4, at : at + 48, :] = buf[0, half, pos].astype(jnp.float32)
                    bf[4, at + 48 : at + span, :] = buf[1, half, pos][: span - 48].astype(jnp.float32)
        for a in range(2 * n, min(2 * n + 2, 5)):
            bc[:, LANES * a : LANES * (a + 1)] = bf[a].astype(jnp.bfloat16)

    def fold(x):
        return jnp.sum(x.reshape(full // 8, 8, LANES), axis=0)

    def product(p, n):
        cols = slice(256 * n, min(256 * n + 256, 5 * LANES))
        return jnp.dot(t[p], bc[:, cols], preferred_element_type=jnp.float32)

    def contract_main():
        for p in range(2):
            late = product(p, 1)
            for b in range(4):
                part = y[p, :, LANES * b : LANES * (b + 1)] if b < 2 else late[:, LANES * (b - 2) : LANES * (b - 1)]
                for a in range(4):
                    acc[p, a, b] = fold(part * bf[a])

    def contract_tail():
        for p in range(2):
            part = product(p, 2)
            for d in range(4):
                acc[p, 4, d] = fold(part * (pltpu.roll(bf[4], TAIL * d, 1) if d else bf[4]))

    for n in range(3):
        start(n)
    after_x(0, 0)
    after_first(0)
    after_x(1, 0)
    after_first(1)
    after_x(2, 0)
    after_first(2)
    after_second(0)
    after_x(0, 1)
    after_second(1)
    after_x(0, 2)
    after_second(2)
    after_x(1, 1)
    for cp in t_copies:
        cp.wait()
    after_c(0)
    after_x(1, 2)
    for p in range(2):
        y[p] = product(p, 0)
    after_c(1)
    contract_main()
    after_c(2)
    contract_tail()

    lane = lax.broadcasted_iota(jnp.int32, (8, LANES), 1)
    wide = lax.broadcasted_iota(jnp.int32, (16, LANES), 1)
    row = lax.broadcasted_iota(jnp.int32, (16, LANES), 0)
    keep = (wide == row) | (wide == 16 + 4 * (row % 4) + row // 4)
    for p in range(2):
        rows = []
        for a in range(4):
            for b in range(4):
                inside = (lane >= TAIL * b) & (lane < TAIL * (b + 1))
                total = acc[p, a, b] + jnp.where(inside, acc[p, 4, (b - a) % 4], 0.0)
                rows.append(jnp.sum(total, axis=0, keepdims=True))
        total = jnp.sum(jnp.concatenate(rows, axis=0), axis=1, keepdims=True)
        mine[p] = jnp.broadcast_to(jnp.sum(jnp.where(keep, total, 0.0), axis=0, keepdims=True), (8, LANES))

    place = oi % 2
    to_vert = remote(mine, from_vert, fs.at[4], fr.at[2, 0], peer)
    sent.append(to_vert)
    for p in range(2):
        remote(mine.at[p], from_pair.at[place, v], fs.at[2 * p + 1], fr.at[place, v], pair(p, 1 - v))

        @pl.when(jnp.logical_not(diag[p]))
        def _(p=p):
            remote(mine.at[p], from_pair.at[place, v], fs.at[2 * p], fr.at[place, v], pair(p, v))

        @pl.when(diag[p])
        def _(p=p):
            pltpu.make_async_copy(mine.at[p], from_pair.at[p, v], fr.at[p, v]).start()

    for cp in small:
        cp.wait()
    energy_i = occ_levels[occ_bins[oi]]
    ea = jnp.zeros((8, LANES), jnp.float32)
    eb = jnp.zeros((8, LANES), jnp.float32)
    for k in range(4):
        level = vir_levels[vir_bins[k]]
        ea = jnp.where(lane // 4 == k, level, ea)
        eb = jnp.where(lane % 4 == k, level, eb)

    to_vert.wait_recv()
    for p in range(2):
        for w in range(2):
            pltpu.make_async_copy(from_pair.at[p, w], from_pair.at[p, w], fr.at[p, w]).wait()
        here = mine[p] + from_vert[p]
        there = from_pair[p, 0] + from_pair[p, 1]
        denom = energy_i + occ_levels[occ_bins[oj * 2 + p]] - ea - eb
        new = (here + pltpu.roll(there, LANES - 16, 1)) / denom
        swapped = (there + pltpu.roll(here, LANES - 16, 1)) / denom
        two = 2.0 * new - swapped

        def spread(x):
            x = jnp.where(v == 0, x, pltpu.roll(x, LANES - 8, 1))
            x = jnp.where(lax.broadcasted_iota(jnp.int32, (8, LANES), 0) == 0, x, pltpu.roll(x, LANES - 4, 1))
            return x[:2, :4]

        out[0, 0, p] = spread(new)
        out[1, 0, p] = spread(swapped)

    for cp in sent:
        cp.wait_send()
    for p in range(2):
        pltpu.make_async_copy(mine.at[p], mine.at[p], fs.at[2 * p + 1]).wait()

        @pl.when(jnp.logical_not(diag[p]))
        def _(p=p):
            pltpu.make_async_copy(mine.at[p], mine.at[p], fs.at[2 * p]).wait()


def on_device(amplitudes, slabs, occ_bins, vir_bins, occ_levels, vir_levels):
    full = amplitudes.shape[2]
    bf16, f32 = jnp.bfloat16, jnp.float32
    dma, vmem = pltpu.SemaphoreType.DMA, pltpu.VMEM
    any_space = pl.BlockSpec(memory_space=pltpu.HBM)
    smem = pltpu.SMEM
    both = pl.pallas_call(
        kernel,
        out_shape=jax.ShapeDtypeStruct((2, 1, 2, 2, 4), f32),
        in_specs=[any_space] * 6,
        out_specs=pl.BlockSpec(memory_space=pltpu.VMEM),
        scratch_shapes=[
            smem(occ_bins.shape, jnp.int32), smem(vir_bins.shape, jnp.int32),
            smem(occ_levels.shape, f32), smem(vir_levels.shape, f32),
            dma((4,)),
            vmem((2, full, full), bf16),
            vmem((slabs.shape[1], slabs.shape[0], slabs.shape[2]), bf16),
            vmem((2, 2, N_Z, 80, LANES), bf16),
            vmem((2, 2, N_Z, 80, LANES), bf16),
            vmem((2, 2, N_Z, 48, LANES), bf16),
            vmem((5, full, LANES), f32),
            vmem((full, 5 * LANES), bf16),
            vmem((2, full, 2 * LANES), f32),
            vmem((2, 5, 4, 8, LANES), f32),
            vmem((2, 8, LANES), f32),
            vmem((2, 8, LANES), f32),
            vmem((2, 2, 8, LANES), f32),
            dma((2,)), dma,
            dma((3, 11)), dma((3, 11)),
            dma((3, 3)), dma((3, 3)),
            dma((3, 5)), dma((3, 5)),
            dma((5,)), dma((3, 2)),
        ],
        compiler_params=pltpu.CompilerParams(
            collective_id=0, has_side_effects=True, vmem_limit_bytes=56 << 20),
    )(amplitudes, jnp.transpose(slabs, (1, 0, 2)), occ_bins, vir_bins, occ_levels, vir_levels)
    return both[0], (2.0 * both[0] - both[1]).astype(bf16)


def solution(mesh):
    return jax.shard_map(
        on_device,
        mesh=mesh,
        in_specs=(P("oi", "oj", None, None), P(None, "oi", None), P(), P(), P(), P()),
        out_specs=(P("oi", "oj", "vert", None), P("oi", "oj", "vert", None)),
        check_vma=False,
    )
```

time: 46 us -> 37.6 us (0.82)
  Pallas kernels: 40.5 us -> 35.6 us
  local copies, waits for them, and re-layouts: 4.73 us -> 0 us
  other arithmetic: 0 us -> 1.26 us
    pallas_call x1, Pallas kernels: 40.5 us -> 35.6 us  [on_device(): pl.pallas_call(kernel, out_shape=jax.ShapeDtypeStruct((2, 1, 2, 2, 4), f3...]
    unnamed x11 -> x0, local copies, waits for them, and re-layouts: 4.73 us -> none
    convert_element_type x0 -> x1, other arithmetic: none -> 1.26 us  [on_device(): return (both[0], (2.0 * both[0] - both[1]).astype(bf16))]
where the time goes in v1:
time: 37.6 us; the launch traced here: 37.5 us
  Pallas kernels  35.6 us (95%)
  other arithmetic  1.26 us (3%)
  between operations  0.64 us (2%)
    pallas_call x1, Pallas kernels, on_device(): pl.pallas_call(kernel, out_shape=jax.ShapeDtypeStruct((2, 1, 2, 2, 4), f3...  35.6 us
    convert_element_type x1, other arithmetic, on_device(): return (both[0], (2.0 * both[0] - both[1]).astype(bf16))  1.26 us

profile of v1, /device:TPU:16, one launch (start us, length us, event | category | flops | bytes accessed | tf_op | source)
XLA Modules:
  0.0 37.5 jit_solution(8397920230366907017)
XLA Ops:
  0.6 35.6 %shard_map.77 = f32[2,1,2,2,4]{4,3,2,1,0:T(2,128)} custom-call(bf16[1,2,1200,1200]{3,2,1,0:T(8,128)(2,1)} %amps.1, bf16[75,4,300]{2,1,0:T(4,128)(2,1)} %bitcast.8, s32[16]{0:T(128)} %occ_bins_in.1, s32[4]{0:T(128)} %vir_bins_in.1, f32[64]{0:T(128)} %occ_levels_in.1, f32[64]{0:T(128)} %vir_levels_in.1), custom_call_target="tpu_custom_call" | custom-call | tf_op jit(solution)/shard_map/pallas_call | solution.py:294
  36.2 1.3 %fusion = (bf16[1,2,2,4]{3,2,1,0:T(2,128)(2,1)}, f32[1,2,2,4]{3,2,1,0:T(2,128)}) fusion(f32[2,1,2,2,4]{4,3,2,1,0:T(2,128)} %shard_map.77), kind=kLoop, calls=%fused_computation.1 | loop fusion | flops 48 | bytes 224 | tf_op jit(solution)/shard_map/convert_element_type | solution.py:324

commit v2 on v1

--- a/solution.py
+++ b/solution.py
@@ -9,7 +9,7 @@
 LANES = 128
 N_Z = 8
 TAIL = 32
-EARLY = (False, False, True)
+EARLY = (False, False, False)
 GROUPS = ((0, 1), (1, 5), (5, 8))
 STEPS = (1, -1, 2, -2)
 
@@ -61,12 +61,6 @@
         cp = pltpu.make_async_copy(src, dst, small_sem.at[k])
         cp.start()
         small.append(cp)
-    t_copies = []
-    for p in range(2):
-        cp = pltpu.make_async_copy(amps.at[0, p], t.at[p], t_sem.at[p])
-        cp.start()
-        t_copies.append(cp)
-
     own_copy.wait()
     wide_own = own[...].astype(jnp.float32)
     lane = lax.broadcasted_iota(jnp.int32, (80, LANES), 1)
@@ -102,7 +96,7 @@
 
     x_copies = [[None] * 3 for _ in bufs]
     c_copies = [[] for _ in bufs]
-    z_first, z_second = [], []
+    z_first, z_second = {}, {}
 
     def to_sibling(n, block):
         k = len(c_copies[n])
@@ -122,7 +116,7 @@
             for k, d in enumerate(STEPS):
                 row.append(send(
                     buf.at[c, xl, 0], buf.at[c, xl, place_of(-d % N_Z)], zs.at[n, 7 + k], zr.at[n, 7 + k], ring(d, 1 - xl)))
-        z_first.append(row)
+        z_first[n] = row
 
     def after_first(n):
         buf = bufs[n]
@@ -136,7 +130,7 @@
             send(buf.at[c, lines, back + c * (ahead - back)], buf.at[c, lines, place_of(4)],
                  zs.at[n, 6], zr.at[n, 6], ring(2 - 4 * c, xl)),
         ]
-        z_second.append(row)
+        z_second[n] = row
         if not EARLY[n]:
             x_send(n, 1)
         to_sibling(n, buf.at[c, lines, pl.ds(1, 4)])
@@ -193,8 +187,13 @@
             for d in range(4):
                 acc[p, 4, d] = fold(part * (pltpu.roll(bf[4], TAIL * d, 1) if d else bf[4]))
 
-    for n in range(3):
+    for n in (0, 1, 2):
         start(n)
+    t_copies = []
+    for p in range(2):
+        cp = pltpu.make_async_copy(amps.at[0, p], t.at[p], t_sem.at[p])
+        cp.start()
+        t_copies.append(cp)
     after_x(0, 0)
     after_first(0)
     after_x(1, 0)
@@ -204,18 +203,20 @@
     after_second(0)
     after_x(0, 1)
     after_second(1)
+    after_x(1, 1)
+    after_second(2)
+    after_x(2, 1)
     after_x(0, 2)
-    after_second(2)
-    after_x(1, 1)
+    after_x(1, 2)
+    after_x(2, 2)
     for cp in t_copies:
         cp.wait()
     after_c(0)
-    after_x(1, 2)
+    after_c(1)
+    after_c(2)
     for p in range(2):
         y[p] = product(p, 0)
-    after_c(1)
     contract_main()
-    after_c(2)
     contract_tail()
 
     lane = lax.broadcasted_iota(jnp.int32, (8, LANES), 1)
@@ -293,7 +294,7 @@
     smem = pltpu.SMEM
     both = pl.pallas_call(
         kernel,
-        out_shape=jax.ShapeDtypeStruct((2, 1, 2, 2, 4), f32),
+        out_shape=pltpu.VMEM((2, 1, 2, 2, 4), f32),
         in_specs=[any_space] * 6,
         out_specs=pl.BlockSpec(memory_space=pltpu.VMEM),
         scratch_shapes=[

time: 37.6 us -> 35.6 us (0.947)
  Pallas kernels: 35.6 us -> 34.3 us
  other arithmetic: 1.26 us -> 0.58 us
    pallas_call x1, Pallas kernels: 35.6 us -> 34.3 us  [on_device(): pl.pallas_call(kernel, out_shape=pltpu.VMEM((2, 1, 2, 2, 4), f32), in_spe...]
    convert_element_type x1, other arithmetic: 1.26 us -> 0.58 us  [on_device(): return (both[0], (2.0 * both[0] - both[1]).astype(bf16))]
where the time goes in v2:
time: 35.6 us; the launch traced here: 35.5 us
  Pallas kernels  34.3 us (96%)
  between operations  0.64 us (2%)
  other arithmetic  0.58 us (2%)
    pallas_call x1, Pallas kernels, on_device(): pl.pallas_call(kernel, out_shape=pltpu.VMEM((2, 1, 2, 2, 4), f32), in_spe...  34.3 us

profile of v2, /device:TPU:16, one launch (start us, length us, event | category | flops | bytes accessed | tf_op | source)
XLA Modules:
  0.0 35.5 jit_solution(6151222330277313714)
XLA Ops:
  0.6 34.3 %shard_map.77 = f32[2,1,2,2,4]{4,3,2,1,0:T(2,128)S(1)} custom-call(bf16[1,2,1200,1200]{3,2,1,0:T(8,128)(2,1)} %amps.1, bf16[75,4,300]{2,1,0:T(4,128)(2,1)} %bitcast.8, s32[16]{0:T(128)} %occ_bins_in.1, s32[4]{0:T(128)} %vir_bins_in.1, f32[64]{0:T(128)} %occ_levels_in.1, f32[64]{0:T(128)} %vir_levels_in.1), custom_call_target="tpu_custom_call" | custom-call | tf_op jit(solution)/shard_map/pallas_call | solution.py:295
  34.9 0.6 %fusion = (bf16[1,2,2,4]{3,2,1,0:T(2,128)(2,1)}, f32[1,2,2,4]{3,2,1,0:T(2,128)}) fusion(f32[2,1,2,2,4]{4,3,2,1,0:T(2,128)S(1)} %shard_map.77), kind=kLoop, calls=%fused_computation.1 | loop fusion | flops 48 | bytes 224 | tf_op jit(solution)/shard_map/convert_element_type | solution.py:325

commit v3 on v2

--- a/solution.py
+++ b/solution.py
@@ -11,7 +11,7 @@
 TAIL = 32
 EARLY = (False, False, False)
 GROUPS = ((0, 1), (1, 5), (5, 8))
-STEPS = (1, -1, 2, -2)
+STEPS = (2, -2, 1, -1)
 
 
 def place_of(r):
@@ -20,7 +20,7 @@
 
 
 def kernel(amps, slabs, occ_bins_in, vir_bins_in, occ_levels_in, vir_levels_in, out,
-           occ_bins, vir_bins, occ_levels, vir_levels, small_sem, t, own, ra, rb, rc, bf, bc, y, acc, mine, from_vert, from_pair,
+           occ_bins, vir_bins, occ_levels, vir_levels, small_sem, t, own, ra, rb, rc, bf, bc, acc, mine, from_vert, from_pair,
            t_sem, own_sem, zs, zr, xs, xr, cs, cr, fs, fr):
     oi, oj, v = lax.axis_index("oi"), lax.axis_index("oj"), lax.axis_index("vert")
     z, xl, yy, c = oi // 2, oi % 2, oj // 2, oj % 2
@@ -120,7 +120,7 @@
 
     def after_first(n):
         buf = bufs[n]
-        for cp in z_first[n]:
+        for cp in z_first[n][:2]:
             cp.wait_recv()
         lines = pl.ds(0, 2) if EARLY[n] else pl.ds(xl, 1)
         back, ahead = place_of(6), place_of(2)
@@ -131,6 +131,8 @@
                  zs.at[n, 6], zr.at[n, 6], ring(2 - 4 * c, xl)),
         ]
         z_second[n] = row
+        for cp in z_first[n][2:]:
+            cp.wait_recv()
         if not EARLY[n]:
             x_send(n, 1)
         to_sibling(n, buf.at[c, lines, pl.ds(1, 4)])
@@ -173,14 +175,6 @@
         cols = slice(256 * n, min(256 * n + 256, 5 * LANES))
         return jnp.dot(t[p], bc[:, cols], preferred_element_type=jnp.float32)
 
-    def contract_main():
-        for p in range(2):
-            late = product(p, 1)
-            for b in range(4):
-                part = y[p, :, LANES * b : LANES * (b + 1)] if b < 2 else late[:, LANES * (b - 2) : LANES * (b - 1)]
-                for a in range(4):
-                    acc[p, a, b] = fold(part * bf[a])
-
     def contract_tail():
         for p in range(2):
             part = product(p, 2)
@@ -194,17 +188,17 @@
         cp = pltpu.make_async_copy(amps.at[0, p], t.at[p], t_sem.at[p])
         cp.start()
         t_copies.append(cp)
-    after_x(0, 0)
     after_first(0)
-    after_x(1, 0)
     after_first(1)
-    after_x(2, 0)
     after_first(2)
     after_second(0)
+    after_second(1)
+    after_second(2)
+    after_x(0, 0)
+    after_x(1, 0)
+    after_x(2, 0)
     after_x(0, 1)
-    after_second(1)
     after_x(1, 1)
-    after_second(2)
     after_x(2, 1)
     after_x(0, 2)
     after_x(1, 2)
@@ -214,9 +208,12 @@
     after_c(0)
     after_c(1)
     after_c(2)
-    for p in range(2):
-        y[p] = product(p, 0)
-    contract_main()
+    for n in range(2):
+        for p in range(2):
+            part = product(p, n)
+            for k in range(2):
+                for a in range(4):
+                    acc[p, a, 2 * n + k] = fold(part[:, LANES * k : LANES * (k + 1)] * bf[a])
     contract_tail()
 
     lane = lax.broadcasted_iota(jnp.int32, (8, LANES), 1)
@@ -234,8 +231,6 @@
         mine[p] = jnp.broadcast_to(jnp.sum(jnp.where(keep, total, 0.0), axis=0, keepdims=True), (8, LANES))
 
     place = oi % 2
-    to_vert = remote(mine, from_vert, fs.at[4], fr.at[2, 0], peer)
-    sent.append(to_vert)
     for p in range(2):
         remote(mine.at[p], from_pair.at[place, v], fs.at[2 * p + 1], fr.at[place, v], pair(p, 1 - v))
 
@@ -246,6 +241,9 @@
         @pl.when(diag[p])
         def _(p=p):
             pltpu.make_async_copy(mine.at[p], from_pair.at[p, v], fr.at[p, v]).start()
+
+    to_vert = remote(mine, from_vert, fs.at[4], fr.at[2, 0], peer)
+    sent.append(to_vert)
 
     for cp in small:
         cp.wait()
@@ -308,7 +306,6 @@
             vmem((2, 2, N_Z, 48, LANES), bf16),
             vmem((5, full, LANES), f32),
             vmem((full, 5 * LANES), bf16),
-            vmem((2, full, 2 * LANES), f32),
             vmem((2, 5, 4, 8, LANES), f32),
             vmem((2, 8, LANES), f32),
             vmem((2, 8, LANES), f32),

time: 35.6 us -> 35.4 us (level)
  no operation moved by 1% of the time
where the time goes in v3:
time: 35.4 us; the launch traced here: 35.3 us
  Pallas kernels  34.1 us (96%)
  between operations  0.64 us (2%)
  other arithmetic  0.58 us (2%)
    pallas_call x1, Pallas kernels, on_device(): pl.pallas_call(kernel, out_shape=pltpu.VMEM((2, 1, 2, 2, 4), f32), in_spe...  34.1 us

profile of v3, /device:TPU:16, one launch (start us, length us, event | category | flops | bytes accessed | tf_op | source)
XLA Modules:
  0.0 35.3 jit_solution(5461395081192675735)
XLA Ops:
  0.6 34.1 %shard_map.77 = f32[2,1,2,2,4]{4,3,2,1,0:T(2,128)S(1)} custom-call(bf16[1,2,1200,1200]{3,2,1,0:T(8,128)(2,1)} %amps.1, bf16[75,4,300]{2,1,0:T(4,128)(2,1)} %bitcast.8, s32[16]{0:T(128)} %occ_bins_in.1, s32[4]{0:T(128)} %vir_bins_in.1, f32[64]{0:T(128)} %occ_levels_in.1, f32[64]{0:T(128)} %vir_levels_in.1), custom_call_target="tpu_custom_call" | custom-call | tf_op jit(solution)/shard_map/pallas_call | solution.py:293
  34.7 0.6 %fusion = (bf16[1,2,2,4]{3,2,1,0:T(2,128)(2,1)}, f32[1,2,2,4]{3,2,1,0:T(2,128)}) fusion(f32[2,1,2,2,4]{4,3,2,1,0:T(2,128)S(1)} %shard_map.77), kind=kLoop, calls=%fused_computation.1 | loop fusion | flops 48 | bytes 224 | tf_op jit(solution)/shard_map/convert_element_type | solution.py:322
